TPU v7x, 32 devices: a whole 2x2x4 slice. The times are simulated.
32 devices in a mesh: row: 4 (over z), col: 8 (over y, x, core).
Axes of the slice: x: 2, y: 2, z: 4, core: 2. Of those that a mesh axis runs over, the one named last changes fastest.
Arguments:
- matrix_real: bfloat16 [128, 16384], P('col', 'row'), may hold values from -0.5 to 0.5
- matrix_imag: bfloat16 [128, 16384], P('col', 'row'), may hold values from -0.5 to 0.5
- valence_index: int32 [128], P('col'), may hold values from 0 to 15
- conduction_index: int32 [128], P('col'), may hold values from 0 to 31
- valence_energy: float32 [16], replicated, may hold values from -1.5 to -0.1
- conduction_energy: float32 [32], replicated, may hold values from 0.1 to 2
- frequency: float32 [2], replicated, may hold values from 0.2 to 2
Outputs:
- chi_real: bfloat16 [2, 16384, 16384], P(None, 'row', 'col')
- chi_imag: bfloat16 [2, 16384, 16384], P(None, 'row', 'col')
All inputs are finite; a program needn't handle non-finite values.
Results may differ from a plain program's by a relative error of at most 0.005.
Values may be sent and summed in bfloat16 or wider, within the bound.
A program may use at most 384 MiB of HBM per device.

v0:
```python
import jax
import jax.numpy as jnp
from jax import lax
from jax.sharding import PartitionSpec as P


def lookup(indices, table):
    count = table.shape[0]
    picks = indices[:, None] == lax.broadcasted_iota(jnp.int32, (1, count), 1)
    return jnp.sum(jnp.where(picks, table[None, :], 0.0), axis=1)


def contract(left_side, right_side):
    return lax.dot_general(
        left_side, right_side, (((0,), (0,)), ((), ())), preferred_element_type=jnp.float32
    )


def on_device(
    matrix_real,
    matrix_imag,
    valence_index,
    conduction_index,
    valence_energy,
    conduction_energy,
    frequency,
):
    all_valence, all_conduction = (
        lax.all_gather(valence_index, "col", axis=0, tiled=True),
        lax.all_gather(conduction_index, "col", axis=0, tiled=True),
    )
    gap = lookup(all_conduction, conduction_energy) - lookup(all_valence, valence_energy)
    spread_real, spread_imag = (
        lax.all_gather(matrix_real, "row", axis=1, tiled=True),
        lax.all_gather(matrix_imag, "row", axis=1, tiled=True),
    )
    column_real, column_imag = (
        lax.all_to_all(spread_real, "col", split_axis=1, concat_axis=0, tiled=True),
        lax.all_to_all(spread_imag, "col", split_axis=1, concat_axis=0, tiled=True),
    )
    width = column_real.shape[1]
    wide_real = column_real.astype(jnp.float32)
    wide_imag = column_imag.astype(jnp.float32)
    upper_parts = []
    lower_parts = []
    for index in range(frequency.shape[0]):
        omega = frequency[index]
        weight = 4.0 * gap / (gap * gap + omega * omega)
        scaled_real = (weight[:, None] * wide_real).astype(jnp.bfloat16)
        scaled_imag = (weight[:, None] * wide_imag).astype(jnp.bfloat16)
        upper_parts.extend([scaled_real, scaled_imag])
        lower_parts.extend([scaled_imag, -scaled_real])
    upper_side = jnp.concatenate(upper_parts, axis=1)
    lower_side = jnp.concatenate(lower_parts, axis=1)
    right_side = jnp.concatenate([upper_side, lower_side], axis=0)
    block_real, block_imag = (
        lax.all_to_all(matrix_real, "col", split_axis=1, concat_axis=0, tiled=True),
        lax.all_to_all(matrix_imag, "col", split_axis=1, concat_axis=0, tiled=True),
    )
    stacked = jnp.concatenate([block_real, block_imag], axis=0)
    joined = contract(lax.all_gather(stacked, "col", axis=1, tiled=True), right_side)
    real_out = []
    imag_out = []
    for index in range(frequency.shape[0]):
        start = 2 * width * index
        real_out.append((-joined[:, start : start + width]).astype(jnp.bfloat16))
        imag_out.append((-joined[:, start + width : start + 2 * width]).astype(jnp.bfloat16))
    return (jnp.stack(real_out, axis=0), jnp.stack(imag_out, axis=0))


def solution(mesh):
    placed = (P("col", "row"), P("col", "row"), P("col"), P("col"), P(), P(), P())
    return jax.shard_map(
        on_device,
        mesh=mesh,
        in_specs=placed,
        out_specs=(P(None, "row", "col"), P(None, "row", "col")),
        check_vma=False,
    )
```

profile of v0, /device:TPU:0, one launch (start us, length us, event | category | flops | bytes accessed | tf_op | source)
XLA Modules:
  0.0 268.5 jit_solution(3806012387116278453)
XLA Ops:
  7.2 1.6 copy.31
  8.7 5.2 %all-to-all-start.1 = ((bf16[16,8,512]{2,0,1:T(8,128)(2,1)}), bf16[16,8,512]{2,0,1:T(8,128)(2,1)S(1)}, u32[]{:S(2)}, u32[]{:S(2)}) async-start(bf16[16,8,512]{2,0,1:T(8,128)(2,1)} %bitcast.53), calls=%async_computation.1 | async-start | bytes 262144 | tf_op jit(solution)/shard_map/all_to_all | solution.py:58
  13.9 0.9 copy.32
  14.9 4.6 %all-to-all-done.1 = bf16[16,8,512]{2,0,1:T(8,128)(2,1)S(1)} async-done(((bf16[16,8,512]{2,0,1:T(8,128)(2,1)}), bf16[16,8,512]{2,0,1:T(8,128)(2,1)S(1)}, u32[]{:S(2)}, u32[]{:S(2)}) %all-to-all-start.1) | async-done | bytes 131104 | tf_op jit(solution)/shard_map/all_to_all | solution.py:58
  19.4 7.9 %all_to_all.64 = bf16[16,8,512]{2,0,1:T(8,128)(2,1)S(1)} all-to-all(bf16[16,8,512]{2,0,1:T(8,128)(2,1)S(1)} %bitcast.59), channel_id=1, replica_groups=mesh['row'=4,'col'=8] {'col'}, dimensions={1} | all-to-all | bytes 262144 | tf_op jit(solution)/shard_map/all_to_all | solution.py:57
  27.3 0.7 pad_maximum_fusion.2
  28.1 16.0 %all_gather.19 = bf16[16,16384]{1,0:T(8,128)(2,1)S(1)} all-gather(bf16[16,4096]{1,0:T(8,128)(2,1)} %param.8), channel_id=1, replica_groups=mesh['row'=4,'col'=8] {'row'}, dimensions={1}, use_global_device_ids=true | all-gather | bytes 655360 | tf_op jit(solution)/shard_map/all_gather | solution.py:35
  44.1 0.8 copy.29
  44.9 3.5 %all-to-all-start.3 = ((bf16[16,8,2048]{2,0,1:T(8,128)(2,1)}), bf16[16,8,2048]{2,0,1:T(8,128)(2,1)S(1)}, u32[]{:S(2)}, u32[]{:S(2)}) async-start(bf16[16,8,2048]{2,0,1:T(8,128)(2,1)} %bitcast.51), calls=%async_computation.3 | async-start | bytes 1048576 | tf_op jit(solution)/shard_map/all_to_all | solution.py:39
  48.4 17.1 %all_gather.18 = bf16[16,16384]{1,0:T(8,128)(2,1)S(1)} all-gather(bf16[16,4096]{1,0:T(8,128)(2,1)} %param.7), channel_id=1, replica_groups=mesh['row'=4,'col'=8] {'row'}, dimensions={1}, use_global_device_ids=true | all-gather | bytes 655360 | tf_op jit(solution)/shard_map/all_gather | solution.py:34
  65.6 1.3 fusion.33
  69.3 0.8 copy.30
  70.1 1.3 dynamic-slice
  72.1 0.9 dynamic-update-slice
  73.0 0.8 dynamic-update-slice.1
  73.8 8.2 %all-reduce.2 = (s32[128]{0:T(128)S(1)}, s32[128]{0:T(128)S(1)}) all-reduce(s32[128]{0:T(128)S(1)} %dynamic-update-slice, s32[128]{0:T(128)S(1)} %dynamic-update-slice.1), channel_id=1, replica_groups=mesh['row'=4,'col'=8] {'col'}, use_global_device_ids=true, to_apply=%add | all-reduce | flops 256 | bytes 2048
  82.0 0.7 select_reduce_fusion
  82.7 0.7 select_reduce_fusion.1
  83.5 4.2 %all-to-all-start.2 = ((bf16[16,8,2048]{2,0,1:T(8,128)(2,1)}), bf16[16,8,2048]{2,0,1:T(8,128)(2,1)}, u32[]{:S(2)}, u32[]{:S(2)}) async-start(bf16[16,8,2048]{2,0,1:T(8,128)(2,1)} %bitcast.52), calls=%async_computation.2 | async-start | bytes 1048576 | tf_op jit(solution)/shard_map/all_to_all | solution.py:38
  87.9 9.5 %all-to-all-done.2 = bf16[16,8,2048]{2,0,1:T(8,128)(2,1)} async-done(((bf16[16,8,2048]{2,0,1:T(8,128)(2,1)}), bf16[16,8,2048]{2,0,1:T(8,128)(2,1)}, u32[]{:S(2)}, u32[]{:S(2)}) %all-to-all-start.2) | async-done | bytes 524320 | tf_op jit(solution)/shard_map/all_to_all | solution.py:38
  97.4 1.4 fusion.29
  98.8 53.9 %fusion.8 = f32[4096,8192]{1,0:T(8,128)} fusion(bf16[256,4096]{1,0:T(8,128)(2,1)} %all-gather.2.cloned.1.call-done, bf16[128,2048]{1,0:T(8,128)(2,1)S(1)} %get-tuple-element.14, bf16[128,2048]{1,0:T(8,128)(2,1)S(1)} %get-tuple-element.13, bf16[128,2048]{1,0:T(8,128)(2,1)S(1)} %get-tuple-element.4, bf16[128,2048]{1,0:T(8,128)(2,1)S(1)} %get-tuple-element.12, ...), kind=kOutput, calls=%fused_computation.14 | convolution fusion | flops 17213423616 | bytes 139460608 | tf_op jit(solution)/shard_map/dot_general | solution.py:14
  152.7 65.2 %fusion.6 = (bf16[1,4096,2048]{2,1,0:T(8,128)(2,1)}, bf16[1,4096,2048]{2,1,0:T(8,128)(2,1)}, bf16[1,4096,2048]{2,1,0:T(8,128)(2,1)}, bf16[1,4096,2048]{2,1,0:T(8,128)(2,1)}) fusion(f32[4096,8192]{1,0:T(8,128)} %fusion.8), kind=kLoop, calls=%fused_computation.12 | loop fusion | flops 67108864 | bytes 201326592 | tf_op jit(solution)/shard_map/stack | solution.py:68
  217.9 43.7 %pad_maximum_fusion = (bf16[2,4096,2048]{2,1,0:T(8,128)(2,1)}, bf16[2,4096,2048]{2,1,0:T(8,128)(2,1)}) fusion(bf16[1,4096,2048]{2,1,0:T(8,128)(2,1)} %get-tuple-element.10, bf16[1,4096,2048]{2,1,0:T(8,128)(2,1)} %get-tuple-element.11, bf16[1,4096,2048]{2,1,0:T(8,128)(2,1)} %get-tuple-element.9, bf16[1,4096,2048]{2,1,0:T(8,128)(2,1)} %get-tuple-element.8), kind=kLoop, calls=%fused_computation.8 | loop fusion | flops 33554432 | bytes 134217728 | tf_op jit(solution)/shard_map/stack | solution.py:68
  (8 shorter events, 0.3 us)
Async XLA Ops:
  8.7 10.7 %all-to-all-start.1 = ((bf16[16,8,512]{2,0,1:T(8,128)(2,1)}), bf16[16,8,512]{2,0,1:T(8,128)(2,1)S(1)}, u32[]{:S(2)}, u32[]{:S(2)}) async-start(bf16[16,8,512]{2,0,1:T(8,128)(2,1)} %bitcast.53), calls=%async_computation.1 | async-start | bytes 262144 | tf_op jit(solution)/shard_map/all_to_all | solution.py:58
  13.9 84.9 %all-gather.2.cloned.1.call-start = ((), (), s32[]{:S(2)}) async-start(), calls=%async_computation.4 | async-start | bytes 2359296 | tf_op jit(solution)/shard_map/all_gather | solution.py:61
  44.9 38.6 %all-to-all-start.3 = ((bf16[16,8,2048]{2,0,1:T(8,128)(2,1)}), bf16[16,8,2048]{2,0,1:T(8,128)(2,1)S(1)}, u32[]{:S(2)}, u32[]{:S(2)}) async-start(bf16[16,8,2048]{2,0,1:T(8,128)(2,1)} %bitcast.51), calls=%async_computation.3 | async-start | bytes 1048576 | tf_op jit(solution)/shard_map/all_to_all | solution.py:39
  83.5 13.9 %all-to-all-start.2 = ((bf16[16,8,2048]{2,0,1:T(8,128)(2,1)}), bf16[16,8,2048]{2,0,1:T(8,128)(2,1)}, u32[]{:S(2)}, u32[]{:S(2)}) async-start(bf16[16,8,2048]{2,0,1:T(8,128)(2,1)} %bitcast.52), calls=%async_computation.2 | async-start | bytes 1048576 | tf_op jit(solution)/shard_map/all_to_all | solution.py:38
Sparse Core Ops, SparseCore 0:
  28.2 30.7 all-gather.1
where the time goes:
time: 269 us; the launch traced here: 268 us
  other arithmetic  113 us (42%)
  matrix products  53.9 us (20%)
  blocking collectives  49.2 us (18%)
  between operations  17.2 us (6%)
  waiting for transfers between devices  14.1 us (5%)
  starting transfers between devices  12.9 us (5%)
  local copies, waits for them, and re-layouts  8.46 us (3%)
    another operation x2, other arithmetic, on_device(): return (jnp.stack(real_out, axis=0), jnp.stack(imag_out, axis=0))  109 us
    dot_general x1, matrix products, contract(): lax.dot_general(left_side, right_side, (((0,), (0,)), ((), ())), preferre...  53.9 us
    all_gather x1, blocking collectives, on_device(): lax.all_gather(matrix_real, 'row', axis=1, tiled=True)  17.1 us
    all_gather x1, blocking collectives, on_device(): lax.all_gather(matrix_imag, 'row', axis=1, tiled=True)  16 us
    all_to_all x1, waiting for transfers between devices, on_device(): lax.all_to_all(spread_real, 'col', split_axis=1, concat_axis=0, tiled=True)  9.51 us
    unnamed x1, blocking collectives  8.18 us
    all_to_all x1, blocking collectives, on_device(): lax.all_to_all(matrix_real, 'col', split_axis=1, concat_axis=0, tiled=True)  7.91 us
  transfers between devices with their start and end apart: 4, of which 2 were waited for; matrix products, arithmetic and copies ran while one was open for 4% of the time, Pallas kernels for 0%

commit v1 on v0

v1 whole, which is shorter than its diff:
```python
import functools

import jax
import jax.numpy as jnp
from jax import lax
from jax.experimental import pallas as pl
from jax.experimental.pallas import tpu as pltpu
from jax.sharding import PartitionSpec as P

MESH = pl.DeviceIdType.MESH
ANY = pl.BlockSpec(memory_space=pl.ANY)
SMEM = pl.BlockSpec(memory_space=pltpu.SMEM)
VMEM = pl.BlockSpec(memory_space=pltpu.VMEM)


def flip(index, mask):
    result = index
    bit = 1
    while bit <= mask:
        if mask & bit:
            result = result + bit * (1 - 2 * ((index // bit) % 2))
        bit *= 2
    return result


def chain_order(cols):
    order = [0, 1]
    evens = list(range(2, cols, 2))
    for even in evens:
        order.append(even)
    for even in evens:
        order.append(even + 1)
    return order


def gather_kernel(
    rows,
    cols,
    real_ref,
    imag_ref,
    valence_ref,
    conduction_ref,
    valence_energy_ref,
    conduction_energy_ref,
    left_ref,
    right_ref,
    gap_ref,
    left_send,
    left_forward,
    left_recv,
    up_send,
    down_send,
    right_recv,
    gap_send,
    gap_recv,
    local_sem,
):
    z = lax.axis_index("row")
    j = lax.axis_index("col")
    pairs = real_ref.shape[0]
    width = right_ref.shape[2]
    per_plane = cols // rows
    home = j // per_plane
    offset = pl.multiple_of((j % per_plane) * width, width)
    sibling = flip(j, 1)
    is_source = z == home
    sends_up = (z >= home) & (z < rows - 1)
    sends_down = (z <= home) & (z > 0)

    barrier = pltpu.get_barrier_semaphore()
    for step in range(1, cols):
        pl.semaphore_signal(
            barrier, inc=1, device_id=(z, flip(j, step)), device_id_type=MESH
        )

    @pl.when(z > 0)
    def _():
        pl.semaphore_signal(barrier, inc=1, device_id=(z - 1, j), device_id_type=MESH)

    @pl.when(z < rows - 1)
    def _():
        pl.semaphore_signal(barrier, inc=1, device_id=(z + 1, j), device_id_type=MESH)

    ends = jnp.where((z == 0) | (z == rows - 1), 1, 2)
    pl.semaphore_wait(barrier, cols - 1 + ends)

    def remote(src, dst, send_sem, recv_sem, device):
        return pltpu.make_async_remote_copy(
            src_ref=src,
            dst_ref=dst,
            send_sem=send_sem,
            recv_sem=recv_sem,
            device_id=device,
            device_id_type=MESH,
        )

    halves = ((real_ref, 0), (imag_ref, pairs))
    directions = ((sends_up, up_send, 1), (sends_down, down_send, -1))

    for sends, send_sem, hop in directions:

        @pl.when(sends & is_source)
        def _(send_sem=send_sem, hop=hop):
            for ref, start in halves:
                remote(
                    ref.at[:, pl.ds(offset, width)],
                    right_ref.at[j, pl.ds(start, pairs), :],
                    send_sem.at[0],
                    right_recv.at[0],
                    (z + hop, j),
                ).start()

    for step in list(range(2, cols, 2)) + [1]:
        for ref, start in halves:
            remote(
                ref,
                left_ref.at[j, pl.ds(start, pairs), :],
                left_send.at[step],
                left_recv.at[step],
                (z, flip(j, step)),
            ).start()

    for ref, start in halves:
        pltpu.make_async_copy(
            ref, left_ref.at[j, pl.ds(start, pairs), :], local_sem.at[0]
        ).start()

    for pair in range(pairs):
        gap = (
            conduction_energy_ref[conduction_ref[pair]]
            - valence_energy_ref[valence_ref[pair]]
        )
        gap_ref[j, pair : pair + 1, :] = jnp.full((1, gap_ref.shape[2]), gap)
    for step in range(1, cols):
        remote(
            gap_ref.at[j],
            gap_ref.at[j],
            gap_send.at[step],
            gap_recv.at[step],
            (z, flip(j, step)),
        ).start()

    def left_wait(step):
        shard = flip(j, step)
        if step == 0:
            pltpu.make_async_copy(
                left_ref.at[shard], left_ref.at[shard], local_sem.at[0]
            ).wait()
        else:
            remote(
                left_ref.at[shard],
                left_ref.at[shard],
                left_send.at[step],
                left_recv.at[step],
                (z, sibling),
            ).wait_recv()

    def hand_on(src, step, sends, send_sem, hop):
        shard = flip(j, step)

        @pl.when(sends)
        def _():
            remote(
                src,
                right_ref.at[shard],
                send_sem.at[step],
                right_recv.at[step],
                (z + hop, j),
            ).start()

    def left_step(step):
        shard = flip(j, step)
        left_wait(step)
        part = left_ref.at[shard, :, pl.ds(offset, width)]
        if step > 0:
            for sends, send_sem, hop in directions:
                hand_on(part, step, sends & is_source, send_sem, hop)
        if step % 2 == 0 and step > 0:
            remote(
                left_ref.at[shard],
                left_ref.at[shard],
                left_forward.at[step],
                left_recv.at[step + 1],
                (z, sibling),
            ).start()

        @pl.when(is_source)
        def _():
            pltpu.make_async_copy(
                part, right_ref.at[shard], right_recv.at[step]
            ).start()

    def right_wait(step):
        shard = flip(j, step)
        pltpu.make_async_copy(
            right_ref.at[shard], right_ref.at[shard], right_recv.at[step]
        ).wait()

    def right_step(step):
        @pl.when(jnp.logical_not(is_source))
        def _():
            right_wait(step)
            for sends, send_sem, hop in directions:
                hand_on(right_ref.at[flip(j, step)], step, sends, send_sem, hop)

    order = chain_order(cols)
    behind = 2
    for position in range(len(order) + behind):
        if position < len(order):
            left_step(order[position])
        if position >= behind:
            right_step(order[position - behind])

    @pl.when(is_source)
    def _():
        for step in range(cols):
            right_wait(step)

    for step in range(1, cols):
        remote(
            gap_ref.at[j], gap_ref.at[flip(j, step)], gap_send.at[step],
            gap_recv.at[step], (z, sibling),
        ).wait()

    def sent(shard_ref, sem):
        remote(shard_ref, shard_ref, sem, left_recv.at[0], (z, sibling)).wait_send()

    for step in range(1, cols):
        if step == 1 or step % 2 == 0:
            sent(left_ref.at[j], left_send.at[step])
        if step % 2 == 0:
            sent(left_ref.at[j], left_forward.at[step])
    for sends, send_sem, hop in directions:

        @pl.when(sends)
        def _(send_sem=send_sem):
            for step in range(cols):
                sent(right_ref.at[j], send_sem.at[step])


def gather(rows, cols, width, matrix_real, matrix_imag, indices):
    pairs, depth = matrix_real.shape
    dma = pltpu.SemaphoreType.DMA((cols,))
    return pl.pallas_call(
        functools.partial(gather_kernel, rows, cols),
        out_shape=(
            jax.ShapeDtypeStruct((cols, 2 * pairs, depth), jnp.bfloat16),
            jax.ShapeDtypeStruct((cols, 2 * pairs, width), jnp.bfloat16),
            jax.ShapeDtypeStruct((cols, pairs, 128), jnp.float32),
        ),
        in_specs=[ANY, ANY, SMEM, SMEM, SMEM, SMEM],
        out_specs=(ANY, ANY, VMEM),
        scratch_shapes=[dma] * 9,
        compiler_params=pltpu.CompilerParams(collective_id=0, has_side_effects=True),
    )(matrix_real, matrix_imag, *indices)


def product_kernel(
    count, pairs, frequency_ref, gap_ref, right_ref, left_ref, real_ref, imag_ref, scaled
):
    cols, both, width = right_ref.shape

    @pl.when(pl.program_id(0) == 0)
    def _():
        def shard_scale(shard, carry):
            gap = gap_ref[shard]
            base = pl.multiple_of(shard * both, both)
            wide_real = right_ref[shard, :pairs, :].astype(jnp.float32)
            wide_imag = right_ref[shard, pairs:, :].astype(jnp.float32)
            for index in range(count):
                omega = frequency_ref[index]
                weight = (4.0 * gap / (gap * gap + omega * omega))[:, :1]
                scaled_real = (weight * wide_real).astype(jnp.bfloat16)
                scaled_imag = (weight * wide_imag).astype(jnp.bfloat16)
                upper = pl.ds(base, pairs)
                lower = pl.ds(base + pairs, pairs)
                scaled[2 * index, upper, :] = -scaled_real
                scaled[2 * index, lower, :] = -scaled_imag
                scaled[2 * index + 1, upper, :] = -scaled_imag
                scaled[2 * index + 1, lower, :] = scaled_real
            return carry

        lax.fori_loop(0, cols, shard_scale, 0)

    left = left_ref[...].reshape(cols * both, left_ref.shape[2])
    left = left.T
    chunk = min(width, 512)
    for index in range(count):
        for part, out_ref in ((0, real_ref), (1, imag_ref)):
            for start in range(0, width, chunk):
                out_ref[index, :, start : start + chunk] = jnp.dot(
                    left,
                    scaled[2 * index + part, :, start : start + chunk],
                    preferred_element_type=jnp.float32,
                ).astype(out_ref.dtype)


def product(frequency, gap, right, left):
    cols, both, depth = left.shape
    width = right.shape[2]
    count = frequency.shape[0]
    tile = 256
    out = jax.ShapeDtypeStruct((count, depth, width), jnp.bfloat16)
    out_spec = pl.BlockSpec((count, tile, width), lambda i: (0, i, 0))
    return pl.pallas_call(
        functools.partial(product_kernel, count, both // 2),
        out_shape=(out, out),
        grid=(depth // tile,),
        in_specs=[
            SMEM,
            pl.BlockSpec(gap.shape, lambda i: (0, 0, 0)),
            pl.BlockSpec(right.shape, lambda i: (0, 0, 0)),
            pl.BlockSpec((cols, both, tile), lambda i: (0, 0, i)),
        ],
        out_specs=(out_spec, out_spec),
        scratch_shapes=[pltpu.VMEM((2 * count, cols * both, width), jnp.bfloat16)],
        compiler_params=pltpu.CompilerParams(vmem_limit_bytes=48 * 1024 * 1024),
    )(frequency, gap, right, left)


def solution(mesh):
    rows, cols = mesh.shape["row"], mesh.shape["col"]

    def on_device(matrix_real, matrix_imag, valence_index, conduction_index,
                  valence_energy, conduction_energy, frequency):
        width = matrix_real.shape[1] * rows // cols
        left, right, gap = gather(
            rows, cols, width, matrix_real, matrix_imag,
            (valence_index, conduction_index, valence_energy, conduction_energy),
        )
        return product(frequency, gap, right, left)

    placed = (P("col", "row"), P("col", "row"), P("col"), P("col"), P(), P(), P())
    return jax.shard_map(
        on_device,
        mesh=mesh,
        in_specs=placed,
        out_specs=(P(None, "row", "col"), P(None, "row", "col")),
        check_vma=False,
    )
```

time: 269 us -> 82.3 us (0.31)
  other arithmetic: 113 us -> 0 us
  Pallas kernels: 0 us -> 77.1 us
  matrix products: 53.9 us -> 0 us
  blocking collectives: 49.2 us -> 0 us
  between operations: 17.2 us -> 0.65 us
  waiting for transfers between devices: 14.1 us -> 0 us
  starting transfers between devices: 12.9 us -> 0 us
  local copies, waits for them, and re-layouts: 8.46 us -> 4.3 us
    another operation x2 -> x0, other arithmetic: 109 us -> none  [on_device(): return (jnp.stack(real_out, axis=0), jnp.stack(imag_out, axis=0))]
    pallas_call x0 -> x2, Pallas kernels: none -> 77.1 us  [the longest x1 47.9 us: gather(): pl.pallas_call(functools.partial(gather_kernel, rows, cols), out_shape=(j...]
    dot_general x1 -> x0, matrix products: 53.9 us -> none  [contract(): lax.dot_general(left_side, right_side, (((0,), (0,)), ((), ())), preferre...]
    all_gather x2 -> x0, blocking collectives: 33.1 us -> none  [the longest x1 17.1 us: on_device(): lax.all_gather(matrix_real, 'row', axis=1, tiled=True)]
    all_to_all x3 -> x0, waiting for transfers between devices: 14.1 us -> none  [the longest x1 9.51 us: on_device(): lax.all_to_all(spread_real, 'col', split_axis=1, concat_axis=0, tiled=True)]
    all_to_all x3 -> x0, starting transfers between devices: 12.8 us -> none  [the longest x1 5.17 us: on_device(): lax.all_to_all(matrix_imag, 'col', split_axis=1, concat_axis=0, tiled=True)]
    unnamed x1 -> x0, blocking collectives: 8.18 us -> none
    all_to_all x1 -> x0, blocking collectives: 7.91 us -> none  [on_device(): lax.all_to_all(matrix_real, 'col', split_axis=1, concat_axis=0, tiled=True)]
  transfers between devices with their start and end apart: 4 -> 0, of which waited for: 2 -> 0; matrix products, arithmetic and copies ran while one was open for 4% -> 0% of each run, Pallas kernels for 0% -> 0%
where the time goes in v1:
time: 82.3 us; the launch traced here: 82.1 us
  Pallas kernels  77.1 us (94%)
  local copies, waits for them, and re-layouts  4.3 us (5%)
    pallas_call x1, Pallas kernels, gather(): pl.pallas_call(functools.partial(gather_kernel, rows, cols), out_shape=(j...  47.9 us
    pallas_call x1, Pallas kernels, product(): pl.pallas_call(functools.partial(product_kernel, count, both // 2), out_s...  29.2 us
    unnamed x8, local copies, waits for them, and re-layouts  4.3 us

profile of v1, /device:TPU:0, one launch (start us, length us, event | category | flops | bytes accessed | tf_op | source)
XLA Modules:
  0.0 82.1 jit_solution(7307143288056676437)
XLA Ops:
  0.6 47.9 %shard_map.86 = (bf16[8,32,4096]{2,1,0:T(8,128)(2,1)}, bf16[8,32,2048]{2,1,0:T(8,128)(2,1)}, f32[8,16,128]{2,1,0:T(8,128)}) custom-call(bf16[16,4096]{1,0:T(8,128)(2,1)} %real_ref.1, bf16[16,4096]{1,0:T(8,128)(2,1)} %imag_ref.1, s32[16]{0:T(128)} %valence_ref.1, s32[16]{0:T(128)} %conduction_ref.1, f32[16]{0:T(128)} %valence_energy_ref.1, ...), custom_call_target="tpu_custom_call" | custom-call | tf_op jit(solution)/shard_map/pallas_call | solution.py:244
  48.5 0.0 copy-start
  48.5 1.6 %copy-done = bf16[8,32,4096]{2,1,0:T(8,128)(2,1)S(1)} copy-done((bf16[8,32,4096]{2,1,0:T(8,128)(2,1)S(1)}, bf16[8,32,4096]{2,1,0:T(8,128)(2,1)}, u32[]{:S(2)}) %copy-start) | copy-done | bytes 2097176
  50.1 0.0 copy-start.1
  50.1 1.2 %copy-done.1 = bf16[8,32,2048]{2,1,0:T(8,128)(2,1)S(1)} copy-done((bf16[8,32,2048]{2,1,0:T(8,128)(2,1)S(1)}, bf16[8,32,2048]{2,1,0:T(8,128)(2,1)}, u32[]{:S(2)}) %copy-start.1) | copy-done | bytes 1048600
  51.3 0.0 copy-start.2
  51.3 0.8 %copy-done.2 = f32[8,16,128]{2,1,0:T(8,128)S(1)} copy-done((f32[8,16,128]{2,1,0:T(8,128)S(1)}, f32[8,16,128]{2,1,0:T(8,128)}, u32[]{:S(2)}) %copy-start.2) | copy-done | bytes 65560
  52.2 0.0 copy-start.3
  52.2 0.7 copy-done.3
  52.8 29.2 %shard_map.87 = (bf16[2,4096,2048]{2,1,0:T(8,128)(2,1)}, bf16[2,4096,2048]{2,1,0:T(8,128)(2,1)}) custom-call(f32[2]{0:T(128)S(1)} %copy-done.3, f32[8,16,128]{2,1,0:T(8,128)S(1)} %copy-done.2, bf16[8,32,2048]{2,1,0:T(8,128)(2,1)S(1)} %copy-done.1, bf16[8,32,4096]{2,1,0:T(8,128)(2,1)S(1)} %copy-done), custom_call_target="tpu_custom_call" | custom-call | tf_op jit(solution)/shard_map/pallas_call | solution.py:305
Async XLA Ops:
  48.5 1.6 %copy-start = (bf16[8,32,4096]{2,1,0:T(8,128)(2,1)S(1)}, bf16[8,32,4096]{2,1,0:T(8,128)(2,1)}, u32[]{:S(2)}) copy-start(bf16[8,32,4096]{2,1,0:T(8,128)(2,1)} %get-tuple-element.7.left_ref) | copy-start | bytes 6291460
  50.1 1.2 %copy-start.1 = (bf16[8,32,2048]{2,1,0:T(8,128)(2,1)S(1)}, bf16[8,32,2048]{2,1,0:T(8,128)(2,1)}, u32[]{:S(2)}) copy-start(bf16[8,32,2048]{2,1,0:T(8,128)(2,1)} %get-tuple-element.6.right_ref) | copy-start | bytes 3145732
  51.3 0.8 %copy-start.2 = (f32[8,16,128]{2,1,0:T(8,128)S(1)}, f32[8,16,128]{2,1,0:T(8,128)}, u32[]{:S(2)}) copy-start(f32[8,16,128]{2,1,0:T(8,128)} %get-tuple-element.5.gap_ref) | copy-start | bytes 196612
  52.2 0.7 copy-start.3

commit v2 on v1

--- a/solution.py
+++ b/solution.py
@@ -8,7 +8,6 @@
 from jax.sharding import PartitionSpec as P
 
 MESH = pl.DeviceIdType.MESH
-ANY = pl.BlockSpec(memory_space=pl.ANY)
 SMEM = pl.BlockSpec(memory_space=pltpu.SMEM)
 VMEM = pl.BlockSpec(memory_space=pltpu.VMEM)
 
@@ -53,7 +52,6 @@
     right_recv,
     gap_send,
     gap_recv,
-    local_sem,
 ):
     z = lax.axis_index("row")
     j = lax.axis_index("col")
@@ -94,35 +92,32 @@
             device_id_type=MESH,
         )
 
-    halves = ((real_ref, 0), (imag_ref, pairs))
     directions = ((sends_up, up_send, 1), (sends_down, down_send, -1))
+    strip = pl.ds(offset, width)
+
+    left_ref[j, :pairs, :] = real_ref[...]
+    left_ref[j, pairs:, :] = imag_ref[...]
+
+    def hand_on(src, step, sends, send_sem, hop):
+        @pl.when(sends)
+        def _():
+            remote(
+                src,
+                right_ref.at[flip(j, step)],
+                send_sem.at[step],
+                right_recv.at[step],
+                (z + hop, j),
+            ).start()
 
     for sends, send_sem, hop in directions:
-
-        @pl.when(sends & is_source)
-        def _(send_sem=send_sem, hop=hop):
-            for ref, start in halves:
-                remote(
-                    ref.at[:, pl.ds(offset, width)],
-                    right_ref.at[j, pl.ds(start, pairs), :],
-                    send_sem.at[0],
-                    right_recv.at[0],
-                    (z + hop, j),
-                ).start()
-
+        hand_on(left_ref.at[j, :, strip], 0, sends & is_source, send_sem, hop)
     for step in list(range(2, cols, 2)) + [1]:
-        for ref, start in halves:
-            remote(
-                ref,
-                left_ref.at[j, pl.ds(start, pairs), :],
-                left_send.at[step],
-                left_recv.at[step],
-                (z, flip(j, step)),
-            ).start()
-
-    for ref, start in halves:
-        pltpu.make_async_copy(
-            ref, left_ref.at[j, pl.ds(start, pairs), :], local_sem.at[0]
+        remote(
+            left_ref.at[j],
+            left_ref.at[j],
+            left_send.at[step],
+            left_recv.at[step],
+            (z, flip(j, step)),
         ).start()
 
     for pair in range(pairs):
@@ -140,13 +135,9 @@
             (z, flip(j, step)),
         ).start()
 
-    def left_wait(step):
+    def left_step(step):
         shard = flip(j, step)
-        if step == 0:
-            pltpu.make_async_copy(
-                left_ref.at[shard], left_ref.at[shard], local_sem.at[0]
-            ).wait()
-        else:
+        if step > 0:
             remote(
                 left_ref.at[shard],
                 left_ref.at[shard],
@@ -154,27 +145,10 @@
                 left_recv.at[step],
                 (z, sibling),
             ).wait_recv()
-
-    def hand_on(src, step, sends, send_sem, hop):
-        shard = flip(j, step)
-
-        @pl.when(sends)
-        def _():
-            remote(
-                src,
-                right_ref.at[shard],
-                send_sem.at[step],
-                right_recv.at[step],
-                (z + hop, j),
-            ).start()
-
-    def left_step(step):
-        shard = flip(j, step)
-        left_wait(step)
-        part = left_ref.at[shard, :, pl.ds(offset, width)]
-        if step > 0:
             for sends, send_sem, hop in directions:
-                hand_on(part, step, sends & is_source, send_sem, hop)
+                hand_on(
+                    left_ref.at[shard, :, strip], step, sends & is_source, send_sem, hop
+                )
         if step % 2 == 0 and step > 0:
             remote(
                 left_ref.at[shard],
@@ -186,9 +160,7 @@
 
         @pl.when(is_source)
         def _():
-            pltpu.make_async_copy(
-                part, right_ref.at[shard], right_recv.at[step]
-            ).start()
+            right_ref[shard] = left_ref[shard, :, strip]
 
     def right_wait(step):
         shard = flip(j, step)
@@ -210,11 +182,6 @@
             left_step(order[position])
         if position >= behind:
             right_step(order[position - behind])
-
-    @pl.when(is_source)
-    def _():
-        for step in range(cols):
-            right_wait(step)
 
     for step in range(1, cols):
         remote(
@@ -248,19 +215,24 @@
             jax.ShapeDtypeStruct((cols, 2 * pairs, width), jnp.bfloat16),
             jax.ShapeDtypeStruct((cols, pairs, 128), jnp.float32),
         ),
-        in_specs=[ANY, ANY, SMEM, SMEM, SMEM, SMEM],
-        out_specs=(ANY, ANY, VMEM),
-        scratch_shapes=[dma] * 9,
-        compiler_params=pltpu.CompilerParams(collective_id=0, has_side_effects=True),
+        in_specs=[VMEM, VMEM, SMEM, SMEM, SMEM, SMEM],
+        out_specs=(VMEM, VMEM, VMEM),
+        scratch_shapes=[dma] * 8,
+        compiler_params=pltpu.CompilerParams(
+            collective_id=0, has_side_effects=True, vmem_limit_bytes=60 * 1024 * 1024
+        ),
     )(matrix_real, matrix_imag, *indices)
 
 
 def product_kernel(
-    count, pairs, frequency_ref, gap_ref, right_ref, left_ref, real_ref, imag_ref, scaled
+    count, pairs, frequency_ref, gap_ref, right_ref, left_ref, real_ref, imag_ref, scaled, turned
 ):
     cols, both, width = right_ref.shape
 
-    @pl.when(pl.program_id(0) == 0)
+    index = pl.program_id(1)
+    start = pl.program_id(2)
+
+    @pl.when((pl.program_id(0) == 0) & (index == 0) & (start == 0))
     def _():
         def shard_scale(shard, carry):
             gap = gap_ref[shard]
@@ -282,39 +254,46 @@
 
         lax.fori_loop(0, cols, shard_scale, 0)
 
-    left = left_ref[...].reshape(cols * both, left_ref.shape[2])
-    left = left.T
-    chunk = min(width, 512)
-    for index in range(count):
-        for part, out_ref in ((0, real_ref), (1, imag_ref)):
-            for start in range(0, width, chunk):
-                out_ref[index, :, start : start + chunk] = jnp.dot(
-                    left,
-                    scaled[2 * index + part, :, start : start + chunk],
-                    preferred_element_type=jnp.float32,
-                ).astype(out_ref.dtype)
+    @pl.when((index == 0) & (start == 0))
+    def _():
+        turned[...] = left_ref[...].reshape(cols * both, left_ref.shape[2]).T
+
+    block = real_ref.shape[2]
+    chunk = 256
+    for part, out_ref in ((0, real_ref), (1, imag_ref)):
+        for place in range(0, block, chunk):
+            columns = pl.ds(pl.multiple_of(start * block + place, chunk), chunk)
+            out_ref[0, :, place : place + chunk] = jnp.dot(
+                turned[...],
+                scaled[2 * index + part, :, columns],
+                preferred_element_type=jnp.float32,
+            ).astype(out_ref.dtype)
 
 
 def product(frequency, gap, right, left):
     cols, both, depth = left.shape
     width = right.shape[2]
     count = frequency.shape[0]
-    tile = 256
+    tile = 1024
+    block = min(width, 1024)
     out = jax.ShapeDtypeStruct((count, depth, width), jnp.bfloat16)
-    out_spec = pl.BlockSpec((count, tile, width), lambda i: (0, i, 0))
+    out_spec = pl.BlockSpec((1, tile, block), lambda i, f, h: (f, i, h))
     return pl.pallas_call(
         functools.partial(product_kernel, count, both // 2),
         out_shape=(out, out),
-        grid=(depth // tile,),
+        grid=(depth // tile, count, width // block),
         in_specs=[
             SMEM,
-            pl.BlockSpec(gap.shape, lambda i: (0, 0, 0)),
-            pl.BlockSpec(right.shape, lambda i: (0, 0, 0)),
-            pl.BlockSpec((cols, both, tile), lambda i: (0, 0, i)),
+            pl.BlockSpec(gap.shape, lambda i, f, h: (0, 0, 0)),
+            pl.BlockSpec(right.shape, lambda i, f, h: (0, 0, 0)),
+            pl.BlockSpec((cols, both, tile), lambda i, f, h: (0, 0, i)),
         ],
         out_specs=(out_spec, out_spec),
-        scratch_shapes=[pltpu.VMEM((2 * count, cols * both, width), jnp.bfloat16)],
-        compiler_params=pltpu.CompilerParams(vmem_limit_bytes=48 * 1024 * 1024),
+        scratch_shapes=[
+            pltpu.VMEM((2 * count, cols * both, width), jnp.bfloat16),
+            pltpu.VMEM((tile, cols * both), jnp.bfloat16),
+        ],
+        compiler_params=pltpu.CompilerParams(vmem_limit_bytes=60 * 1024 * 1024),
     )(frequency, gap, right, left)
 
 

time: 82.3 us -> 70.2 us (0.85)
  the two profiles are of different devices: /device:TPU:0 before, /device:TPU:6 now
where the time goes in v2:
time: 70.2 us; the launch traced here: 69.9 us
  Pallas kernels  69.3 us (99%)
    pallas_call x1, Pallas kernels, gather(): pl.pallas_call(functools.partial(gather_kernel, rows, cols), out_shape=(j...  42.7 us
    pallas_call x1, Pallas kernels, product(): pl.pallas_call(functools.partial(product_kernel, count, both // 2), out_s...  26.5 us

profile of v2, /device:TPU:6, one launch (start us, length us, event | category | flops | bytes accessed | tf_op | source)
XLA Modules:
  0.0 69.9 jit_solution(14788635401312768792)
XLA Ops:
  0.6 42.7 %shard_map.86 = (bf16[8,32,4096]{2,1,0:T(8,128)(2,1)}, bf16[8,32,2048]{2,1,0:T(8,128)(2,1)}, f32[8,16,128]{2,1,0:T(8,128)}) custom-call(bf16[16,4096]{1,0:T(8,128)(2,1)} %real_ref.1, bf16[16,4096]{1,0:T(8,128)(2,1)} %imag_ref.1, s32[16]{0:T(128)} %valence_ref.1, s32[16]{0:T(128)} %conduction_ref.1, f32[16]{0:T(128)} %valence_energy_ref.1, ...), custom_call_target="tpu_custom_call" | custom-call | tf_op jit(solution)/shard_map/pallas_call | solution.py:211
  43.4 26.5 %shard_map.87 = (bf16[2,4096,2048]{2,1,0:T(8,128)(2,1)}, bf16[2,4096,2048]{2,1,0:T(8,128)(2,1)}) custom-call(f32[2]{0:T(128)} %frequency_ref.1, f32[8,16,128]{2,1,0:T(8,128)} %get-tuple-element.5.gap_ref, bf16[8,32,2048]{2,1,0:T(8,128)(2,1)} %get-tuple-element.6.right_ref, bf16[8,32,4096]{2,1,0:T(8,128)(2,1)} %get-tuple-element.7.left_ref), custom_call_target="tpu_custom_call" | custom-call | tf_op jit(solution)/shard_map/pallas_call | solution.py:281

commit v3 on v2

v3 whole, which is shorter than its diff:
```python
import functools

import jax
import jax.numpy as jnp
from jax import lax
from jax.experimental import pallas as pl
from jax.experimental.pallas import tpu as pltpu
from jax.sharding import PartitionSpec as P

MESH = pl.DeviceIdType.MESH
SMEM = pl.BlockSpec(memory_space=pltpu.SMEM)
VMEM = pl.BlockSpec(memory_space=pltpu.VMEM)


def flip(index, mask):
    result = index
    bit = 1
    while bit <= mask:
        if mask & bit:
            result = result + bit * (1 - 2 * ((index // bit) % 2))
        bit *= 2
    return result


def gather_kernel(
    rows,
    cols,
    real_ref,
    imag_ref,
    valence_ref,
    conduction_ref,
    valence_energy_ref,
    conduction_energy_ref,
    turned_ref,
    right_ref,
    gap_ref,
    left_ref,
    line_ref,
    left_send,
    left_forward,
    left_recv,
    up_send,
    down_send,
    line_recv,
    right_send,
    right_recv,
    gap_send,
    gap_recv,
):
    z = lax.axis_index("row")
    j = lax.axis_index("col")
    pairs, depth = real_ref.shape
    width = right_ref.shape[2]
    per_plane = cols // rows
    home = j // per_plane
    sibling = flip(j, 1)

    barrier = pltpu.get_barrier_semaphore()
    for step in range(1, cols):
        pl.semaphore_signal(
            barrier, inc=1, device_id=(z, flip(j, step)), device_id_type=MESH
        )

    @pl.when(z > 0)
    def _():
        pl.semaphore_signal(barrier, inc=1, device_id=(z - 1, j), device_id_type=MESH)

    @pl.when(z < rows - 1)
    def _():
        pl.semaphore_signal(barrier, inc=1, device_id=(z + 1, j), device_id_type=MESH)

    line_ref[z, :pairs, :] = real_ref[...]
    line_ref[z, pairs:, :] = imag_ref[...]
    left_ref[j, :pairs, :] = real_ref[...]
    left_ref[j, pairs:, :] = imag_ref[...]

    ends = jnp.where((z == 0) | (z == rows - 1), 1, 2)
    pl.semaphore_wait(barrier, cols - 1 + ends)

    def remote(src, dst, send_sem, recv_sem, device):
        return pltpu.make_async_remote_copy(
            src_ref=src,
            dst_ref=dst,
            send_sem=send_sem,
            recv_sem=recv_sem,
            device_id=device,
            device_id_type=MESH,
        )

    def hand_on(plane, strip, send_sem, hop, allowed):
        part = line_ref.at[plane, :, strip * width : (strip + 1) * width]
        slot = plane * per_plane + strip

        @pl.when(allowed)
        def _():
            remote(
                part, part, send_sem.at[slot], line_recv.at[slot], (z + hop, j)
            ).start()

    for strip in range(per_plane):
        hand_on(z, strip, up_send, 1, z < rows - 1)
        hand_on(z, strip, down_send, -1, z > 0)
    for step in list(range(2, cols, 2)) + [1]:
        remote(
            left_ref.at[j],
            left_ref.at[j],
            left_send.at[step],
            left_recv.at[step],
            (z, flip(j, step)),
        ).start()

    for pair in range(pairs):
        gap = (
            conduction_energy_ref[conduction_ref[pair]]
            - valence_energy_ref[valence_ref[pair]]
        )
        gap_ref[j, pair : pair + 1, :] = jnp.full((1, gap_ref.shape[2]), gap)
    for step in range(1, cols):
        remote(
            gap_ref.at[j],
            gap_ref.at[j],
            gap_send.at[step],
            gap_recv.at[step],
            (z, flip(j, step)),
        ).start()

    def line_step(distance):
        for strip in range(per_plane):
            for hop, send_sem in ((1, up_send), (-1, down_send)):
                plane = z - hop * distance

                @pl.when((plane >= 0) & (plane < rows))
                def _(strip=strip, hop=hop, send_sem=send_sem, plane=plane):
                    slot = plane * per_plane + strip
                    lanes = slice(strip * width, (strip + 1) * width)
                    part = line_ref.at[plane, :, lanes]
                    remote(
                        part, part, send_sem.at[slot], line_recv.at[slot], (z, sibling)
                    ).wait_recv()
                    hand_on(
                        plane, strip, send_sem, hop, (z + hop >= 0) & (z + hop < rows)
                    )

                    @pl.when(slot == j)
                    def _():
                        right_ref[j] = line_ref[plane, :, lanes]

                    @pl.when(slot != j)
                    def _():
                        remote(
                            part,
                            right_ref.at[j],
                            right_send.at[slot],
                            right_recv.at[j],
                            (z, slot),
                        ).start()

    def left_wait(step):
        shard = flip(j, step)
        part = left_ref.at[shard]
        remote(
            part, part, left_send.at[step], left_recv.at[step], (z, sibling)
        ).wait_recv()
        if step % 2 == 0:
            remote(
                part,
                part,
                left_forward.at[step],
                left_recv.at[step + 1],
                (z, sibling),
            ).start()

    for distance in range(1, rows - 1):
        line_step(distance)
    for step in range(2, cols, 2):
        left_wait(step)
    line_step(rows - 1)
    for step in range(1, cols, 2):
        left_wait(step)

    tile = 512

    def turn(index, carry):
        lanes = pl.ds(pl.multiple_of(index * tile, tile), tile)
        block = left_ref[:, :, lanes].reshape(cols * 2 * pairs, tile)
        turned_ref[lanes, :] = block.T
        return carry

    lax.fori_loop(0, depth // tile, turn, 0)

    @pl.when(z == home)
    def _():
        lanes = pl.ds(pl.multiple_of((j % per_plane) * width, width), width)
        for shard in range(cols):
            right_ref[shard] = left_ref[shard, :, lanes]

    @pl.when(z != home)
    def _():
        for step in range(1, cols):
            shard = flip(j, step)
            remote(
                right_ref.at[shard],
                right_ref.at[shard],
                right_send.at[0],
                right_recv.at[shard],
                (z, sibling),
            ).wait_recv()

    for step in range(1, cols):
        remote(
            gap_ref.at[j], gap_ref.at[flip(j, step)], gap_send.at[step],
            gap_recv.at[step], (z, sibling),
        ).wait()

    def sent(shard_ref, sem):
        remote(shard_ref, shard_ref, sem, left_recv.at[0], (z, sibling)).wait_send()

    for step in range(1, cols):
        if step == 1 or step % 2 == 0:
            sent(left_ref.at[j], left_send.at[step])
        if step % 2 == 0:
            sent(left_ref.at[j], left_forward.at[step])
    for plane in range(rows):
        for strip in range(per_plane):
            slot = plane * per_plane + strip

            @pl.when((plane <= z) & (z < rows - 1))
            def _(slot=slot):
                sent(right_ref.at[j], up_send.at[slot])

            @pl.when((plane >= z) & (z > 0))
            def _(slot=slot):
                sent(right_ref.at[j], down_send.at[slot])

            @pl.when((plane != z) & (slot != j))
            def _(slot=slot):
                sent(right_ref.at[j], right_send.at[slot])


def gather(rows, cols, width, matrix_real, matrix_imag, indices):
    pairs, depth = matrix_real.shape
    dma = pltpu.SemaphoreType.DMA((cols,))
    return pl.pallas_call(
        functools.partial(gather_kernel, rows, cols),
        out_shape=(
            jax.ShapeDtypeStruct((depth, cols * 2 * pairs), jnp.bfloat16),
            jax.ShapeDtypeStruct((cols, 2 * pairs, width), jnp.bfloat16),
            jax.ShapeDtypeStruct((cols, pairs, 128), jnp.float32),
        ),
        in_specs=[VMEM, VMEM, SMEM, SMEM, SMEM, SMEM],
        out_specs=(VMEM, VMEM, VMEM),
        scratch_shapes=[
            pltpu.VMEM((cols, 2 * pairs, depth), jnp.bfloat16),
            pltpu.VMEM((rows, 2 * pairs, depth), jnp.bfloat16),
        ]
        + [dma] * 10,
        compiler_params=pltpu.CompilerParams(
            collective_id=0, has_side_effects=True, vmem_limit_bytes=60 * 1024 * 1024
        ),
    )(matrix_real, matrix_imag, *indices)


def product_kernel(
    pairs, frequency_ref, gap_ref, right_ref, turned_ref, real_ref, imag_ref, scaled
):
    cols, both, width = right_ref.shape
    index = pl.program_id(1)
    start = pl.program_id(2)

    @pl.when(pl.program_id(0) == 0)
    def _():
        block = real_ref.shape[2]
        columns = pl.ds(pl.multiple_of(start * block, block), block)
        omega = frequency_ref[index]
        for shard in range(cols):
            gap = gap_ref[shard]
            weight = (4.0 * gap / (gap * gap + omega * omega))[:, :1]
            wide_real = right_ref[shard, :pairs, columns].astype(jnp.float32)
            wide_imag = right_ref[shard, pairs:, columns].astype(jnp.float32)
            scaled_real = (weight * wide_real).astype(jnp.bfloat16)
            scaled_imag = (weight * wide_imag).astype(jnp.bfloat16)
            upper = slice(shard * both, shard * both + pairs)
            lower = slice(shard * both + pairs, (shard + 1) * both)
            scaled[2 * index, upper, columns] = -scaled_real
            scaled[2 * index, lower, columns] = -scaled_imag
            scaled[2 * index + 1, upper, columns] = -scaled_imag
            scaled[2 * index + 1, lower, columns] = scaled_real

    block = real_ref.shape[2]
    chunk = 256
    for part, out_ref in ((0, real_ref), (1, imag_ref)):
        for place in range(0, block, chunk):
            columns = pl.ds(pl.multiple_of(start * block + place, chunk), chunk)
            out_ref[0, :, place : place + chunk] = jnp.dot(
                turned_ref[...],
                scaled[2 * index + part, :, columns],
                preferred_element_type=jnp.float32,
            ).astype(out_ref.dtype)


def product(frequency, gap, right, turned):
    cols, both, width = right.shape
    depth = turned.shape[0]
    count = frequency.shape[0]
    tile = 1024
    block = min(width, 1024)
    out = jax.ShapeDtypeStruct((count, depth, width), jnp.bfloat16)
    out_spec = pl.BlockSpec((1, tile, block), lambda i, f, h: (f, i, h))
    return pl.pallas_call(
        functools.partial(product_kernel, both // 2),
        out_shape=(out, out),
        grid=(depth // tile, count, width // block),
        in_specs=[
            SMEM,
            pl.BlockSpec(gap.shape, lambda i, f, h: (0, 0, 0)),
            pl.BlockSpec(right.shape, lambda i, f, h: (0, 0, 0)),
            pl.BlockSpec((tile, cols * both), lambda i, f, h: (i, 0)),
        ],
        out_specs=(out_spec, out_spec),
        scratch_shapes=[
            pltpu.VMEM((2 * count, cols * both, width), jnp.bfloat16),
        ],
        compiler_params=pltpu.CompilerParams(vmem_limit_bytes=60 * 1024 * 1024),
    )(frequency, gap, right, turned)


def solution(mesh):
    rows, cols = mesh.shape["row"], mesh.shape["col"]

    def on_device(matrix_real, matrix_imag, valence_index, conduction_index,
                  valence_energy, conduction_energy, frequency):
        width = matrix_real.shape[1] * rows // cols
        turned, right, gap = gather(
            rows, cols, width, matrix_real, matrix_imag,
            (valence_index, conduction_index, valence_energy, conduction_energy),
        )
        return product(frequency, gap, right, turned)

    placed = (P("col", "row"), P("col", "row"), P("col"), P("col"), P(), P(), P())
    return jax.shard_map(
        on_device,
        mesh=mesh,
        in_specs=placed,
        out_specs=(P(None, "row", "col"), P(None, "row", "col")),
        check_vma=False,
    )
```

time: 70.2 us -> 63.7 us (0.907)
  the two profiles are of different devices: /device:TPU:6 before, /device:TPU:25 now
where the time goes in v3:
time: 63.7 us; the launch traced here: 63.5 us
  Pallas kernels  62.9 us (99%)
  between operations  0.64 us (1%)
    pallas_call x1, Pallas kernels, gather(): pl.pallas_call(functools.partial(gather_kernel, rows, cols), out_shape=(j...  34.7 us
    pallas_call x1, Pallas kernels, product(): pl.pallas_call(functools.partial(product_kernel, both // 2), out_shape=(o...  28.2 us

profile of v3, /device:TPU:25, one launch (start us, length us, event | category | flops | bytes accessed | tf_op | source)
XLA Modules:
  0.0 63.5 jit_solution(16673150251459329476)
XLA Ops:
  0.6 34.7 %shard_map.86 = (bf16[4096,256]{1,0:T(8,128)(2,1)}, bf16[8,32,2048]{2,1,0:T(8,128)(2,1)}, f32[8,16,128]{2,1,0:T(8,128)}) custom-call(bf16[16,4096]{1,0:T(8,128)(2,1)} %real_ref.1, bf16[16,4096]{1,0:T(8,128)(2,1)} %imag_ref.1, s32[16]{0:T(128)} %valence_ref.1, s32[16]{0:T(128)} %conduction_ref.1, f32[16]{0:T(128)} %valence_energy_ref.1, f32[32]{0:T(128)} %conduction_energy_ref.1), custom_call_target="tpu_custom_call" | custom-call | tf_op jit(solution)/shard_map/pallas_call | solution.py:243
  35.3 28.2 %shard_map.87 = (bf16[2,4096,2048]{2,1,0:T(8,128)(2,1)}, bf16[2,4096,2048]{2,1,0:T(8,128)(2,1)}) custom-call(f32[2]{0:T(128)} %frequency_ref.1, f32[8,16,128]{2,1,0:T(8,128)} %get-tuple-element.5.gap_ref, bf16[8,32,2048]{2,1,0:T(8,128)(2,1)} %get-tuple-element.6.right_ref, bf16[4096,256]{1,0:T(8,128)(2,1)} %get-tuple-element.7.turned_ref), custom_call_target="tpu_custom_call" | custom-call | tf_op jit(solution)/shard_map/pallas_call | solution.py:309
